TPU v7x, 512 devices: a whole 4x4x16 slice. The times are simulated.
512 devices in a mesh: owner: 128 (over x, z, core), col: 4 (over y).
Axes of the slice: x: 4, y: 4, z: 16, core: 2. Of those that a mesh axis runs over, the one named last changes fastest.
Arguments:
- embeddings: bfloat16 [131072, 256], P(('owner', 'col')), may hold values from -6 to 6
- adjacency: bfloat16 [131072, 4096], P('owner', 'col'), may hold values from 0 to 0.021972656
- upd_vals: bfloat16 [131072, 256], P(('owner', 'col')), may hold values from 0 to 0.087890625
- upd_dest: int32 [131072, 1], P(('owner', 'col')), may hold values from 0 to 127; in each aligned block of 256 rows (0 to 255, 256 to 511, ...) at most 4 rows name the same one
- upd_target: int32 [131072], P(('owner', 'col')), may hold values from 0 to 4095
- upd_count: int32 [512], P(('owner', 'col')), may hold values from 64 to 256, as said below
- send_row: int32 [262144], P(('owner', 'col')), may hold values from 0 to 255
- send_dest: int32 [262144, 1], P(('owner', 'col')), may hold values from 0 to 127; in each aligned block of 512 rows (0 to 511, 512 to 1023, ...) at most 8 rows name the same one
- affected: int32 [512], P(('owner', 'col')), may hold values 0 or 1
- w_self: bfloat16 [256, 256], replicated, may hold values from -0.375 to 0.375
- w_inter: bfloat16 [256, 256], replicated, may hold values from -0.375 to 0.375
Outputs:
- refreshed: bfloat16 [131072, 256], P(('owner', 'col'))
Inputs may be any that keep to these rules, and one draw needn't show every extreme that they name: `upd_dest`: among the update rows of one device at most 4 name the same owner; in some device exactly 4 do. `send_dest`: among the sends of one device at most 8 name the same owner; in some device exactly 8 do. `upd_count`: some device has all 256 update rows live.
All inputs are finite; a program needn't handle non-finite values. No bound on the sum of `affected` on one device may be relied on, other than what follows from the above.
Results may differ from a plain program's by a relative error of at most 0.015.
Values may be sent and summed in bfloat16 or wider, within the bound.
A program may use at most 64 MiB of HBM per device.

v0:
```python
import jax
import jax.numpy as jnp
from jax import lax
from jax.sharding import PartitionSpec as P


def slot_positions(target_owner, is_live, owners, capacity):
    onehot = jnp.logical_and(
        target_owner[:, None] == jnp.arange(owners, dtype=jnp.int32)[None, :], is_live[:, None]
    ).astype(jnp.int32)
    running = jnp.cumsum(onehot, axis=0) - 1
    slot_rank = jnp.sum(running * onehot, axis=1)
    return jnp.where(is_live, target_owner * capacity + slot_rank, owners * capacity)


def per_device(
    embeddings,
    adjacency,
    upd_vals,
    upd_dest,
    upd_target,
    upd_count,
    send_row,
    send_dest,
    affected,
    w_self,
    w_inter,
):
    owners = lax.axis_size("owner")
    width = embeddings.shape[1]
    sent_count = send_row.shape[0]
    halo_cap = 2 * sent_count // owners
    upd_rows = upd_vals.shape[0]
    upd_cap = 2 * upd_rows // owners
    tile_width = upd_vals.shape[1]
    row_count = adjacency.shape[0] * adjacency.shape[1] // tile_width
    send_slots = slot_positions(
        send_dest[:, 0], jnp.ones((sent_count,), jnp.bool_), owners, halo_cap
    )
    outgoing = (
        jnp.zeros((owners * halo_cap, width), jnp.bfloat16)
        .at[send_slots]
        .set(embeddings[send_row], mode="drop")
    )
    is_live = jnp.arange(upd_rows, dtype=jnp.int32) < upd_count[0]
    upd_slots = slot_positions(upd_dest[:, 0], is_live, owners, upd_cap)
    bucket_vals = (
        jnp.zeros((owners * upd_cap, tile_width), jnp.bfloat16)
        .at[upd_slots]
        .set(upd_vals, mode="drop")
    )
    bucket_targets = (
        jnp.full((owners * upd_cap,), row_count, jnp.int32)
        .at[upd_slots]
        .set(upd_target, mode="drop")
    )
    got_vals, got_targets = (
        lax.all_to_all(bucket_vals, "owner", split_axis=0, concat_axis=0, tiled=True),
        lax.all_to_all(bucket_targets, "owner", split_axis=0, concat_axis=0, tiled=True),
    )
    tile_rows = adjacency.reshape(row_count, tile_width)
    delta_sum = (
        jnp.zeros((row_count, tile_width), jnp.float32)
        .at[got_targets]
        .add(got_vals.astype(jnp.float32), mode="drop")
    )
    new_rows = (tile_rows.astype(jnp.float32) + delta_sum).astype(jnp.bfloat16)
    new_tile = new_rows.reshape(adjacency.shape)
    received = lax.all_to_all(outgoing, "owner", split_axis=0, concat_axis=0, tiled=True)
    partial_value = jnp.dot(new_tile, received, preferred_element_type=jnp.float32).astype(
        jnp.bfloat16
    )
    neighbours = lax.psum_scatter(
        lax.optimization_barrier(partial_value).astype(jnp.float32).astype(jnp.bfloat16),
        "col",
        scatter_dimension=0,
        tiled=True,
    ).astype(jnp.float32)
    emb_wide = embeddings.astype(jnp.float32)
    self_sum = (neighbours + emb_wide).astype(jnp.bfloat16)
    inter = (neighbours * emb_wide).astype(jnp.bfloat16)
    preact = jnp.dot(self_sum, w_self, preferred_element_type=jnp.float32) + jnp.dot(
        inter, w_inter, preferred_element_type=jnp.float32
    )
    layer_out = jnp.where(preact >= 0, preact, 0.2 * preact).astype(jnp.bfloat16)
    return jnp.where(affected[0] > 0, layer_out, embeddings)


def solution(mesh):
    in_specs = (
        P(("owner", "col"), None),
        P("owner", "col"),
        P(("owner", "col"), None),
        P(("owner", "col"), None),
        P(("owner", "col")),
        P(("owner", "col")),
        P(("owner", "col")),
        P(("owner", "col"), None),
        P(("owner", "col")),
        P(),
        P(),
    )
    out_specs = P(("owner", "col"), None)
    return jax.shard_map(
        per_device, mesh=mesh, in_specs=in_specs, out_specs=out_specs, check_vma=False
    )
```

profile of v0, /device:TPU:1, one launch (start us, length us, event | category | flops | bytes accessed | tf_op | source)
XLA Modules:
  0.0 150.4 jit_solution(737759136782557376)
XLA Ops:
  7.3 0.8 copy.18
  8.1 0.3 fusion.12
  8.5 0.1 add_add_fusion.1
  8.6 0.9 fusion.15
  9.5 0.7 compare_select_fusion.3
  10.2 1.6 %scatter_custom_fusion = s32[512]{0:T(512)S(1)} fusion(s32[256]{0:T(256)S(1)} %bitcast.47, s32[256]{0:T(256)} %param.15, s32[]{:T(128)} %constant.14.clone.1), kind=kCustom, calls=%fused_computation.49 | custom fusion | bytes 2560 | tf_op jit(solution)/shard_map/scatter | solution.py:55
  11.7 0.7 all_to_all.22
  12.5 20.4 %all-to-all-start = ((s32[128,4,1]{1,2,0:T(1,128)}), s32[128,4,1]{1,2,0:T(1,128)S(1)}, u32[]{:S(2)}, u32[]{:S(2)}) async-start(s32[128,4,1]{1,2,0:T(1,128)} %bitcast.9), calls=%async_computation | async-start | bytes 131072 | tf_op jit(solution)/shard_map/all_to_all | solution.py:59
  32.9 0.8 copy.21
  33.7 0.2 fusion.8
  33.9 2.0 %scatter_custom_fusion.1 = bf16[512,256]{1,0:T(8,128)(2,1)S(1)} fusion(s32[256]{0:T(256)S(1)} %bitcast.48, bf16[256,256]{1,0:T(8,128)(2,1)} %param.13, bf16[]{:T(256)} %constant.10.clone.1), kind=kCustom, calls=%fused_computation.31 | custom fusion | bytes 262656 | tf_op jit(solution)/shard_map/scatter | solution.py:50
  36.0 0.8 all_to_all.25
  36.7 11.1 %all-to-all-done = s32[128,4,1]{1,2,0:T(1,128)S(1)} async-done(((s32[128,4,1]{1,2,0:T(1,128)}), s32[128,4,1]{1,2,0:T(1,128)S(1)}, u32[]{:S(2)}, u32[]{:S(2)}) %all-to-all-start) | async-done | bytes 2080 | tf_op jit(solution)/shard_map/all_to_all | solution.py:59
  47.9 6.6 %all-to-all-start.1 = ((bf16[128,4,256]{2,1,0:T(4,128)(2,1)}), bf16[128,4,256]{2,1,0:T(4,128)(2,1)S(1)}, u32[]{:S(2)}, u32[]{:S(2)}) async-start(bf16[128,4,256]{2,1,0:T(4,128)(2,1)} %all_to_all.25), calls=%async_computation.1 | async-start | bytes 524288 | tf_op jit(solution)/shard_map/all_to_all | solution.py:58
  54.5 0.1 add_add_fusion
  54.6 0.2 fusion.5
  54.9 4.6 %scatter_custom_fusion.3 = bf16[1024,256]{1,0:T(8,128)(2,1)} fusion(s32[512]{0:T(512)S(1)} %bitcast.46, bf16[256,256]{1,0:T(8,128)(2,1)S(1)} %copy-done.2, s32[1024]{0:T(1024)S(1)} %pad_clamp_fusion, bf16[]{:T(256)} %constant.10.clone.1), kind=kCustom, calls=%fused_computation.17 | custom fusion | bytes 524290 | tf_op jit(solution)/shard_map/scatter | solution.py:43
  59.4 17.6 %all-to-all-done.1 = bf16[128,4,256]{2,1,0:T(4,128)(2,1)S(1)} async-done(((bf16[128,4,256]{2,1,0:T(4,128)(2,1)}), bf16[128,4,256]{2,1,0:T(4,128)(2,1)S(1)}, u32[]{:S(2)}, u32[]{:S(2)}) %all-to-all-start.1) | async-done | bytes 262176 | tf_op jit(solution)/shard_map/all_to_all | solution.py:58
  77.0 7.5 %all-to-all-start.2 = ((bf16[128,8,256]{2,1,0:T(8,128)(2,1)}), bf16[128,8,256]{2,1,0:T(8,128)(2,1)S(1)}, u32[]{:S(2)}, u32[]{:S(2)}) async-start(bf16[128,8,256]{2,1,0:T(8,128)(2,1)} %bitcast.18), calls=%async_computation.2 | async-start | bytes 1048576 | tf_op jit(solution)/shard_map/all_to_all | solution.py:69
  84.5 0.0 reduce-scatter.2.cloned.1.call-start
  84.6 2.9 %reshape.100 = f32[4096,256]{1,0:T(8,128)} reshape(bf16[1024,1024]{1,0:T(8,128)(2,1)S(1)} %copy-done.1) | data formatting | bytes 6291456 | tf_op jit(solution)/shard_map/convert_element_type | solution.py:67
  87.5 0.5 broadcast.123
  88.0 0.8 reduce.3
  88.8 0.1 all_to_all.24
  89.0 7.1 %scatter_fusion = f32[4096,256]{1,0:T(8,128)} fusion(f32[4096,256]{1,0:T(8,128)} %reshape.100, s32[512]{0:T(512)S(1)} %bitcast.44, f32[512,256]{1,0:T(8,128)S(1)} %reshape.130), kind=kCustom, calls=%fused_computation.3 | custom fusion | flops 131072 | bytes 1574912 | tf_op jit(solution)/shard_map/scatter-add | solution.py:65
  96.1 2.4 %convert_element_type.50 = bf16[4096,256]{1,0:T(8,128)(2,1)S(1)} convert(f32[4096,256]{1,0:T(8,128)} %scatter_fusion) | non-fusion elementwise | flops 1048576 | bytes 6291456 | tf_op jit(solution)/shard_map/convert_element_type | solution.py:67
  98.5 2.6 %reshape.98 = bf16[1024,1024]{1,0:T(8,128)(2,1)} reshape(bf16[4096,256]{1,0:T(8,128)(2,1)S(1)} %convert_element_type.50) | data formatting | bytes 4194304 | tf_op jit(solution)/shard_map/reshape | solution.py:68
  101.1 16.8 %all-to-all-done.2 = bf16[128,8,256]{2,1,0:T(8,128)(2,1)S(1)} async-done(((bf16[128,8,256]{2,1,0:T(8,128)(2,1)}), bf16[128,8,256]{2,1,0:T(8,128)(2,1)S(1)}, u32[]{:S(2)}, u32[]{:S(2)}) %all-to-all-start.2) | async-done | bytes 524320 | tf_op jit(solution)/shard_map/all_to_all | solution.py:69
  117.8 3.1 %convolution_convert_fusion = bf16[1024,256]{1,0:T(8,128)(2,1)} fusion(bf16[1024,1024]{1,0:T(8,128)(2,1)} %reshape.98, bf16[128,8,256]{2,1,0:T(8,128)(2,1)S(1)} %all-to-all-done.2), kind=kOutput, calls=%fused_computation.5 | convolution fusion | flops 537133056 | bytes 3145728 | tf_op jit(solution)/shard_map/dot_general | solution.py:70
  121.6 19.0 %reduce-scatter.2.cloned.1.call-done = bf16[256,256]{1,0:T(8,128)(2,1)} async-done(((bf16[1024,256]{1,0:T(8,128)(2,1)}), bf16[256,256]{1,0:T(8,128)(2,1)}) %reduce-scatter.2.cloned.1.call-update) | async-done | bytes 131088 | tf_op jit(solution)/shard_map/reduce_scatter | solution.py:73
  140.6 1.1 fusion.13
  141.7 1.8 %fusion.2 = bf16[256,256]{1,0:T(8,128)(2,1)} fusion(bf16[256,256]{1,0:T(8,128)(2,1)S(1)} %copy-done.2, f32[256,256]{1,0:T(8,128)S(1)} %fusion.13, bf16[256,256]{1,0:T(8,128)(2,1)S(1)} %copy-done.5, bf16[256,256]{1,0:T(8,128)(2,1)} %reduce-scatter.2.cloned.1.call-done, pred[]{:T(512)} %bitcast), kind=kOutput, calls=%fused_computation.10 | convolution fusion | flops 34209792 | bytes 786433 | tf_op jit(solution)/shard_map/dot_general | solution.py:82
  (28 shorter events, 0.2 us)
Async XLA Ops:
  6.5 134.1 %copy-start = (bf16[256,256]{1,0:T(8,128)(2,1)S(1)}, bf16[256,256]{1,0:T(8,128)(2,1)}, u32[]{:S(2)}) copy-start(bf16[256,256]{1,0:T(8,128)(2,1)} %param.20) | copy-start | bytes 393220
  6.5 48.1 %copy-start.3 = (s32[512,1]{0,1:T(1,128)S(1)}, s32[512,1]{0,1:T(1,128)}, u32[]{:S(2)}) copy-start(s32[512,1]{0,1:T(1,128)} %param.18) | copy-start | bytes 6148
  6.5 48.0 %copy-start.4 = (s32[512]{0:T(512)S(1)}, s32[512]{0:T(512)}, u32[]{:S(2)}) copy-start(s32[512]{0:T(512)} %param.17) | copy-start | bytes 6148
  7.3 47.6 %copy-start.2 = (bf16[256,256]{1,0:T(8,128)(2,1)S(1)}, bf16[256,256]{1,0:T(8,128)(2,1)}, u32[]{:S(2)}) copy-start(bf16[256,256]{1,0:T(8,128)(2,1)} %param.11) | copy-start | bytes 393220
  12.5 35.4 %all-to-all-start = ((s32[128,4,1]{1,2,0:T(1,128)}), s32[128,4,1]{1,2,0:T(1,128)S(1)}, u32[]{:S(2)}, u32[]{:S(2)}) async-start(s32[128,4,1]{1,2,0:T(1,128)} %bitcast.9), calls=%async_computation | async-start | bytes 131072 | tf_op jit(solution)/shard_map/all_to_all | solution.py:59
  33.9 50.7 %copy-start.1 = (bf16[1024,1024]{1,0:T(8,128)(2,1)S(1)}, bf16[1024,1024]{1,0:T(8,128)(2,1)}, u32[]{:S(2)}) copy-start(bf16[1024,1024]{1,0:T(8,128)(2,1)} %param.12) | copy-start | bytes 6291460
  47.9 29.2 %all-to-all-start.1 = ((bf16[128,4,256]{2,1,0:T(4,128)(2,1)}), bf16[128,4,256]{2,1,0:T(4,128)(2,1)S(1)}, u32[]{:S(2)}, u32[]{:S(2)}) async-start(bf16[128,4,256]{2,1,0:T(4,128)(2,1)} %all_to_all.25), calls=%async_computation.1 | async-start | bytes 524288 | tf_op jit(solution)/shard_map/all_to_all | solution.py:58
  77.0 40.8 %all-to-all-start.2 = ((bf16[128,8,256]{2,1,0:T(8,128)(2,1)}), bf16[128,8,256]{2,1,0:T(8,128)(2,1)S(1)}, u32[]{:S(2)}, u32[]{:S(2)}) async-start(bf16[128,8,256]{2,1,0:T(8,128)(2,1)} %bitcast.18), calls=%async_computation.2 | async-start | bytes 1048576 | tf_op jit(solution)/shard_map/all_to_all | solution.py:69
  84.5 56.1 %reduce-scatter.2.cloned.1.call-start = ((), (), s32[]{:S(2)}) async-start(), calls=%async_computation.4 | async-start | bytes 655360 | tf_op jit(solution)/shard_map/reduce_scatter | solution.py:73
  101.1 40.7 %copy-start.5 = (bf16[256,256]{1,0:T(8,128)(2,1)S(1)}, bf16[256,256]{1,0:T(8,128)(2,1)}, u32[]{:S(2)}) copy-start(bf16[256,256]{1,0:T(8,128)(2,1)} %param.21) | copy-start | bytes 393220
Sparse Core Ops, SparseCore 0:
  121.1 19.5 reduce-scatter.1
where the time goes:
time: 152 us; the launch traced here: 150 us
  waiting for transfers between devices  64.6 us (42%)
  starting transfers between devices  34.5 us (23%)
  local copies, waits for them, and re-layouts  17.5 us (12%)
  between operations  15 us (10%)
  other arithmetic  12.9 us (8%)
  matrix products  5.96 us (4%)
    all_to_all x1, starting transfers between devices, per_device(): lax.all_to_all(bucket_targets, 'owner', split_axis=0, concat_axis=0, tile...  20.4 us
    reduce_scatter x1, waiting for transfers between devices, per_device(): lax.psum_scatter(lax.optimization_barrier(partial_value).astype(jnp.float...  19 us
    all_to_all x1, waiting for transfers between devices, per_device(): lax.all_to_all(bucket_vals, 'owner', split_axis=0, concat_axis=0, tiled=T...  17.6 us
    all_to_all x1, waiting for transfers between devices, per_device(): lax.all_to_all(outgoing, 'owner', split_axis=0, concat_axis=0, tiled=True)  16.8 us
    all_to_all x1, waiting for transfers between devices, per_device(): lax.all_to_all(bucket_targets, 'owner', split_axis=0, concat_axis=0, tile...  11.1 us
    all_to_all x1, starting transfers between devices, per_device(): lax.all_to_all(outgoing, 'owner', split_axis=0, concat_axis=0, tiled=True)  7.47 us
    scatter-add x1, other arithmetic, per_device(): delta_sum = jnp.zeros((row_count, tile_width), jnp.float32).at[got_target...  7.11 us
    all_to_all x1, starting transfers between devices, per_device(): lax.all_to_all(bucket_vals, 'owner', split_axis=0, concat_axis=0, tiled=T...  6.56 us
  transfers between devices with their start and end apart: 4, of which 4 were waited for; matrix products, arithmetic and copies ran while one was open for 16% of the time, Pallas kernels for 0%

commit v1 on v0

v1 whole, which is shorter than its diff:
```python
import functools

import jax
import jax.numpy as jnp
from jax import lax
from jax.experimental import pallas as pl
from jax.experimental.pallas import tpu as pltpu
from jax.sharding import PartitionSpec as P

MESH = pl.DeviceIdType.MESH
BF16, F32, I32 = jnp.bfloat16, jnp.float32, jnp.int32
NX, NZ, NK, NC = 4, 16, 2, 4
NQ = NX * NK
OWNERS = NX * NZ * NK
CAPR, CAPU = 8, 4
D = 256
NL = 1024
ORDER = [8] + [s * d for d in range(7, 0, -1) for s in (1, -1)] + [0]
UGRP, HGRP = 4, 2


def owner_of(x, z, k):
    return (x * NZ + z) * NK + k


def iota(shape, dim):
    return lax.broadcasted_iota(I32, shape, dim)


def dot(a, b):
    return jnp.dot(a, b, preferred_element_type=F32)


def dot_t(a, b):
    return lax.dot_general(a, b, (((1,), (1,)), ((), ())), preferred_element_type=F32)


def ranks(dest, live):
    n = dest.shape[1]
    hot = iota((OWNERS, n), 0) == dest
    if live is not None:
        hot = jnp.logical_and(hot, live)
    hot = jnp.where(hot, 1.0, 0.0)
    before = jnp.where(iota((n, n), 0) < iota((n, n), 1), 1.0, 0.0).astype(BF16)
    running = dot(hot.astype(BF16), before)
    return jnp.sum(running * hot, axis=0, keepdims=True).astype(I32)


def split_owner(dest):
    z = jnp.bitwise_and(jnp.right_shift(dest, 1), NZ - 1)
    q = jnp.right_shift(dest, 5) * NK + jnp.bitwise_and(dest, 1)
    return z, q


def onehot(rows, lane_index):
    return jnp.where(iota((rows, lane_index.shape[1]), 0) == lane_index, 1.0, 0.0).astype(BF16)


def kernel(
    cnt, aff, emb, adj, uval, udst, utgt, srow, sdst, ws, wi,
    out,
    tile, us, uz, ur, ts, tz, tr, hs, hz, hr, halo, tmat, ps, pr, own,
    adj_sem, us_s, ts_s, hs_s, uz_r, tz_r, hz_r, loc,
    ur_s, tr_s, hr_s, ur_r, tr_r, hr_r, loc2, p_s, p_r,
):
    me, c = lax.axis_index("owner"), lax.axis_index("col")
    x, z, k = me // (NZ * NK), lax.rem(me // NK, NZ), lax.rem(me, NK)
    q = x * NK + k

    def zdev(step, sign):
        return (owner_of(x, lax.rem(z + sign * ORDER[step] + NZ, NZ), k), c)

    def qdev(i):
        return lax.rem(x + i // NK, NX), lax.rem(k + i % NK, NK)

    adj_copy = pltpu.make_async_copy(adj, tile, adj_sem)
    adj_copy.start()

    barrier = pltpu.get_barrier_semaphore()
    greeted = [zdev(s, 1) for s in range(NZ - 1)]
    for i in range(1, NQ):
        xx, kk = qdev(i)
        greeted.append((owner_of(xx, z, kk), c))
    greeted += [(me, lax.rem(c + i, NC)) for i in range(1, NC)]
    for dev in greeted:
        pl.semaphore_signal(barrier, inc=1, device_id=dev, device_id_type=MESH)

    dest = udst[...]
    live = iota(dest.shape, 1) < cnt[0]
    rank = ranks(dest, live)
    zz, qq = split_owner(dest)
    slot = jnp.where(live, zz * (NQ * 8) + qq * 8 + rank, -8)
    slot2 = jnp.concatenate([slot, slot + CAPU], axis=1)
    vals = uval[...]
    stacked = jnp.concatenate([vals[:, :128], vals[:, 128:]], axis=0)
    us[...] = dot(onehot(NZ * NQ * 8, slot2), stacked).astype(BF16).reshape(NZ, NQ, 8, 128)
    tgt = utgt[...] + 1
    row_z = jnp.where(jnp.logical_and(iota((NZ, dest.shape[1]), 0) == zz, live), 1.0, 0.0)
    lane_q = onehot(128, qq * CAPU + rank)
    hi = (row_z * jnp.right_shift(tgt, 6).astype(F32)).astype(BF16)
    lo = (row_z * jnp.bitwise_and(tgt, 63).astype(F32)).astype(BF16)
    sent_targets = (dot_t(hi, lane_q) * 64.0 + dot_t(lo, lane_q)).astype(I32)
    for i in range(NZ):
        ts[i] = sent_targets[i : i + 1]

    pl.semaphore_wait(barrier, len(greeted))

    def zcopy(src, dst, send, recv, step):
        dev = zdev(step, 1)
        return pltpu.make_async_remote_copy(
            src.at[lax.rem(z + ORDER[step] + NZ, NZ)], dst.at[step], send, recv.at[step],
            device_id=dev, device_id_type=MESH,
        )

    ucopies = [zcopy(us, uz, us_s, uz_r, s) for s in range(NZ - 1)]
    tcopies = [zcopy(ts, tz, ts_s, tz_r, s) for s in range(NZ - 1)]
    for s in range(NZ - 1):
        tcopies[s].start()
        ucopies[s].start()
    locals_ = [
        pltpu.make_async_copy(us.at[z], uz.at[NZ - 1], loc.at[0]),
        pltpu.make_async_copy(ts.at[z], tz.at[NZ - 1], loc.at[1]),
    ]
    for copy in locals_:
        copy.start()

    dest = sdst[...]
    rank = ranks(dest, None)
    zz, qq = split_owner(dest)
    place = onehot(OWNERS * CAPR, zz * (NQ * CAPR) + qq * CAPR + rank)
    pick = dot_t(place, onehot(D, srow[...])).astype(BF16)
    rows = dot(pick, emb[...]).reshape(OWNERS, CAPR, D)
    hs[...] = (
        jnp.concatenate([rows[:, :, :128], rows[:, :, 128:]], axis=1)
        .astype(BF16)
        .reshape(NZ, NQ, 2 * CAPR, 128)
    )
    hcopies = [zcopy(hs, hz, hs_s, hz_r, s) for s in range(NZ - 1)]
    for s in range(NZ - 1):
        hcopies[s].start()
    locals_.append(pltpu.make_async_copy(hs.at[z], hz.at[NZ - 1], loc.at[2]))
    locals_[2].start()

    def forward(src, dst, send, recv, grp, g, copies, local):
        steps = pl.ds(g, grp)
        for s in range(g, g + grp):
            if s < NZ - 1:
                copies[s].wait_recv()
            else:
                local.wait()
        for i in (3, 5, 2, 4, 6, 7, 1):
            xx, kk = qdev(i)
            pltpu.make_async_remote_copy(
                src.at[steps, xx * NK + kk], dst.at[q, steps], send, recv.at[g // grp],
                device_id=(owner_of(xx, z, kk), c), device_id_type=MESH,
            ).start()

    for s in range(NZ - 1):
        tcopies[s].wait_recv()
    locals_[1].wait()
    for i in range(1, NQ):
        xx, kk = qdev(i)
        pltpu.make_async_remote_copy(
            tz, tr.at[q], tr_s, tr_r, device_id=(owner_of(xx, z, kk), c), device_id_type=MESH
        ).start()
    own_t = pltpu.make_async_copy(tz, tr.at[q], loc2.at[0])
    own_t.start()
    for g in range(0, NZ, UGRP):
        forward(uz, ur, ur_s, ur_r, UGRP, g, ucopies, locals_[0])
    own_u = pltpu.make_async_copy(uz.at[:, q], ur.at[q], loc2.at[1])
    own_u.start()

    own_t.wait()
    some = tr.at[pl.ds(0, NQ - 1)]
    pltpu.make_async_copy(some, some, tr_r).wait()
    pltpu.make_async_copy(some, some, tr_s).wait()
    own_u.wait()
    for g in range(NZ // UGRP):
        some = ur.at[pl.ds(0, NQ - 1), pl.ds(g * UGRP, UGRP)]
        pltpu.make_async_copy(some, some, ur_r.at[g]).wait()
    some = ur.at[pl.ds(0, NQ - 1)]
    pltpu.make_async_copy(some, some, ur_s).wait()

    for i in range(OWNERS):
        tmat[i : i + 1] = tr[i // NZ, i % NZ]
    got = tmat[...].astype(F32)
    eye = iota((128, 128), 0) == iota((128, 128), 1)
    lanes = []
    for s in range(CAPU):
        column = jnp.sum(jnp.where(iota((128, 128), 1) == q * CAPU + s, got, 0.0), axis=1, keepdims=True)
        lanes.append(jnp.sum(jnp.where(eye, column, 0.0), axis=0, keepdims=True))
    target = jnp.concatenate(lanes, axis=1).astype(I32) - 1
    packed = ur[...].reshape(OWNERS * 8, 128)
    u_row = iota((OWNERS * CAPU, OWNERS * 8), 0)
    u_from = jnp.bitwise_and(u_row, 127) * 8 + jnp.right_shift(u_row, 7)
    m_col = iota((OWNERS * CAPU, OWNERS * 8), 1)
    halves = [
        dot(jnp.where(m_col == u_from + h * CAPU, 1.0, 0.0).astype(BF16), packed) for h in (0, 1)
    ]
    values = jnp.concatenate(halves, axis=1).astype(BF16)

    adj_copy.wait()
    for j in range(4):
        row_of = jnp.where(jnp.bitwise_and(target, 3) == j, jnp.right_shift(target, 2), -1)
        row_of = jnp.where(target < 0, -1, row_of)

        @pl.loop(0, NL // 256)
        def _(b, j=j, row_of=row_of):
            at = (pl.ds(pl.multiple_of(b * 256, 256), 256), pl.ds(j * 256, 256))
            delta = dot(onehot(256, row_of - b * 256), values)
            tile[at] = (tile[at].astype(F32) + delta).astype(BF16)

    for g in range(0, NZ, HGRP):
        forward(hz, hr, hr_s, hr_r, HGRP, g, hcopies, locals_[2])
    own_h = pltpu.make_async_copy(hz.at[:, q], hr.at[q], loc2.at[2])
    own_h.start()
    own_h.wait()
    for g in range(NZ // HGRP):
        some = hr.at[pl.ds(0, NQ - 1), pl.ds(g * HGRP, HGRP)]
        pltpu.make_async_copy(some, some, hr_r.at[g]).wait()
        for s in range(g * HGRP, (g + 1) * HGRP):
            zs = lax.rem(z - ORDER[s] + NZ, NZ)
            for xs in range(NX):
                a = hr[xs * NK, s].astype(F32)
                b = hr[xs * NK + 1, s].astype(F32)
                at = pl.ds(pl.multiple_of((xs * NZ + zs) * 16, 16), 16)
                halo[at, 0:128] = jnp.concatenate([a[:8], b[:8]], axis=0).astype(BF16)
                halo[at, 128:256] = jnp.concatenate([a[8:], b[8:]], axis=0).astype(BF16)

    for i in (2, 1, 3, 0):
        cc = lax.rem(c + i, NC)
        block = tile[pl.ds(pl.multiple_of(cc * 256, 256), 256), :]
        share = dot(block, halo[...]).astype(BF16)
        if i == 0:
            own[...] = share
        else:
            ps[i - 1] = share
            pltpu.make_async_remote_copy(
                ps.at[i - 1], pr.at[i - 1], p_s, p_r, device_id=(me, cc), device_id_type=MESH
            ).start()

    some = hr.at[pl.ds(0, NQ - 1)]
    pltpu.make_async_copy(some, some, hr_s).wait()
    for src, sem in ((us, us_s), (ts, ts_s), (hs, hs_s)):
        some = src.at[pl.ds(0, NZ - 1)]
        pltpu.make_async_copy(some, some, sem).wait()
    pltpu.make_async_copy(pr, pr, p_r).wait()

    neighbours = own[...].astype(F32)
    for i in range(NC - 1):
        neighbours = neighbours + pr[i].astype(F32)
    wide = emb[...].astype(F32)
    self_sum = (neighbours + wide).astype(BF16)
    inter = (neighbours * wide).astype(BF16)
    preact = dot(self_sum, ws[...]) + dot(inter, wi[...])
    layer = jnp.where(preact >= 0, preact, 0.2 * preact)
    out[...] = jnp.where(aff[0] > 0, layer, wide).astype(BF16)
    pltpu.make_async_copy(ps, ps, p_s).wait()


def per_device(
    embeddings, adjacency, upd_vals, upd_dest, upd_target, upd_count,
    send_row, send_dest, affected, w_self, w_inter,
):
    v = pl.BlockSpec(memory_space=pltpu.VMEM)
    s = pl.BlockSpec(memory_space=pltpu.SMEM)
    a = pl.BlockSpec(memory_space=pl.ANY)
    vm = pltpu.VMEM
    dma = pltpu.SemaphoreType.DMA
    u, r = upd_dest.shape[0], send_dest.shape[0]
    return pl.pallas_call(
        kernel,
        out_shape=jax.ShapeDtypeStruct((D, D), BF16),
        in_specs=[s, s, v, a, v, v, v, v, v, v, v],
        out_specs=v,
        scratch_shapes=[
            vm((NL, NL), BF16),
            vm((NZ, NQ, 8, 128), BF16),
            vm((NZ, NQ, 8, 128), BF16),
            vm((NQ, NZ, 8, 128), BF16),
            vm((NZ, 1, 128), I32),
            vm((NZ, 1, 128), I32),
            vm((NQ, NZ, 1, 128), I32),
            vm((NZ, NQ, 16, 128), BF16),
            vm((NZ, NQ, 16, 128), BF16),
            vm((NQ, NZ, 16, 128), BF16),
            vm((OWNERS * CAPR, D), BF16),
            vm((128, 128), I32),
            vm((NC - 1, 256, 256), BF16),
            vm((NC - 1, 256, 256), BF16),
            vm((256, 256), BF16),
            dma, dma, dma, dma, dma((NZ,)), dma((NZ,)), dma((NZ,)), dma((3,)),
            dma, dma, dma, dma((NZ // UGRP,)), dma, dma((NZ // HGRP,)), dma((3,)), dma, dma,
        ],
        compiler_params=pltpu.CompilerParams(
            collective_id=0, has_side_effects=True, vmem_limit_bytes=48 * 2**20
        ),
    )(
        upd_count, affected, embeddings, adjacency, upd_vals,
        upd_dest.reshape(1, u), upd_target.reshape(1, u),
        send_row.reshape(1, r), send_dest.reshape(1, r), w_self, w_inter,
    )


def solution(mesh):
    rows = P(("owner", "col"))
    wide = P(("owner", "col"), None)
    return jax.shard_map(
        per_device,
        mesh=mesh,
        in_specs=(wide, P("owner", "col"), wide, wide, rows, rows, rows, wide, rows, P(), P()),
        out_specs=wide,
        check_vma=False,
    )
```

time: 152 us -> 77.5 us (0.51)
  Pallas kernels: 0 us -> 67.3 us
  waiting for transfers between devices: 64.6 us -> 0 us
  starting transfers between devices: 34.5 us -> 0 us
  between operations: 15 us -> 1.32 us
  other arithmetic: 12.9 us -> 0 us
  local copies, waits for them, and re-layouts: 17.5 us -> 8.58 us
  matrix products: 5.96 us -> 0 us
    pallas_call x0 -> x1, Pallas kernels: none -> 67.3 us  [per_device(): pl.pallas_call(kernel, out_shape=jax.ShapeDtypeStruct((D, D), BF16), in_s...]
    all_to_all x3 -> x0, waiting for transfers between devices: 45.5 us -> none  [the longest x1 17.6 us: per_device(): lax.all_to_all(bucket_vals, 'owner', split_axis=0, concat_axis=0, tiled=T...]
    all_to_all x3 -> x0, starting transfers between devices: 34.4 us -> none  [the longest x1 20.4 us: per_device(): lax.all_to_all(bucket_targets, 'owner', split_axis=0, concat_axis=0, tile...]
    reduce_scatter x1 -> x0, waiting for transfers between devices: 19 us -> none  [per_device(): lax.psum_scatter(lax.optimization_barrier(partial_value).astype(jnp.float...]
    unnamed x12 -> x19, local copies, waits for them, and re-layouts: 0.03 us -> 8.58 us
    scatter x3 -> x0, local copies, waits for them, and re-layouts: 8.16 us -> none  [the longest x1 4.57 us: per_device(): outgoing = jnp.zeros((owners * halo_cap, width), jnp.bfloat16).at[send_sl...]
    scatter-add x1 -> x0, other arithmetic: 7.11 us -> none  [per_device(): delta_sum = jnp.zeros((row_count, tile_width), jnp.float32).at[got_target...]
    dot_general x3 -> x0, matrix products: 5.96 us -> none  [the longest x1 3.1 us: per_device(): jnp.dot(new_tile, received, preferred_element_type=jnp.float32)]
  transfers between devices with their start and end apart: 4 -> 0, of which waited for: 4 -> 0; matrix products, arithmetic and copies ran while one was open for 16% -> 0% of each run, Pallas kernels for 0% -> 0%
where the time goes in v1:
time: 77.5 us; the launch traced here: 77.2 us
  Pallas kernels  67.3 us (87%)
  local copies, waits for them, and re-layouts  8.58 us (11%)
  between operations  1.32 us (2%)
    pallas_call x1, Pallas kernels, per_device(): pl.pallas_call(kernel, out_shape=jax.ShapeDtypeStruct((D, D), BF16), in_s...  67.3 us
    unnamed x19, local copies, waits for them, and re-layouts  8.58 us

profile of v1, /device:TPU:1, one launch (start us, length us, event | category | flops | bytes accessed | tf_op | source)
XLA Modules:
  0.0 77.2 jit_solution(7123914624479559474)
XLA Ops:
  1.3 0.0 copy-start
  1.3 1.6 %copy-done = bf16[1024,1024]{1,0:T(8,128)(2,1)S(1)} copy-done((bf16[1024,1024]{1,0:T(8,128)(2,1)S(1)}, bf16[1024,1024]{1,0:T(8,128)(2,1)}, u32[]{:S(2)}) %copy-start) | copy-done | bytes 2097176
  2.9 0.0 copy-start.1
  2.9 0.9 %copy-done.1 = bf16[256,256]{1,0:T(8,128)(2,1)S(1)} copy-done((bf16[256,256]{1,0:T(8,128)(2,1)S(1)}, bf16[256,256]{1,0:T(8,128)(2,1)}, u32[]{:S(2)}) %copy-start.1) | copy-done | bytes 131096
  3.8 0.0 copy-start.2
  3.8 0.9 %copy-done.2 = bf16[256,256]{1,0:T(8,128)(2,1)S(1)} copy-done((bf16[256,256]{1,0:T(8,128)(2,1)S(1)}, bf16[256,256]{1,0:T(8,128)(2,1)}, u32[]{:S(2)}) %copy-start.2) | copy-done | bytes 131096
  4.7 0.0 copy-start.3
  4.7 0.9 %copy-done.3 = bf16[256,256]{1,0:T(8,128)(2,1)S(1)} copy-done((bf16[256,256]{1,0:T(8,128)(2,1)S(1)}, bf16[256,256]{1,0:T(8,128)(2,1)}, u32[]{:S(2)}) %copy-start.3) | copy-done | bytes 131096
  5.6 0.0 copy-start.4
  5.6 0.9 %copy-done.4 = bf16[256,256]{1,0:T(8,128)(2,1)S(1)} copy-done((bf16[256,256]{1,0:T(8,128)(2,1)S(1)}, bf16[256,256]{1,0:T(8,128)(2,1)}, u32[]{:S(2)}) %copy-start.4) | copy-done | bytes 131096
  6.5 0.0 copy-start.5
  6.5 0.7 copy-done.5
  7.2 0.0 copy-start.6
  7.2 0.7 copy-done.6
  7.9 0.0 copy-start.7
  7.9 0.7 copy-done.7
  8.6 0.0 copy-start.8
  8.6 0.7 copy-done.8
  9.2 67.3 %shard_map.109 = bf16[256,256]{1,0:T(8,128)(2,1)S(1)} custom-call(s32[1]{0:T(128)S(6)} %copy.13.cnt, s32[1]{0:T(128)S(6)} %copy.14.aff, bf16[256,256]{1,0:T(8,128)(2,1)S(1)} %copy-done.1, bf16[1024,1024]{1,0:T(8,128)(2,1)S(1)} %copy-done, bf16[256,256]{1,0:T(8,128)(2,1)S(1)} %copy-done.2, s32[1,256]{1,0:T(1,128)S(1)} %bitcast.6, s32[1,256]{1,0:T(1,128)S(1)} %bitcast.7, ...), custom_call_target="tpu_custom_call" | custom-call | tf_op jit(solution)/shard_map/pallas_call | solution.py:271
  76.5 0.7 copy.15
Async XLA Ops:
  1.3 1.6 %copy-start = (bf16[1024,1024]{1,0:T(8,128)(2,1)S(1)}, bf16[1024,1024]{1,0:T(8,128)(2,1)}, u32[]{:S(2)}) copy-start(bf16[1024,1024]{1,0:T(8,128)(2,1)} %adj.1) | copy-start | bytes 6291460
  2.9 0.9 %copy-start.1 = (bf16[256,256]{1,0:T(8,128)(2,1)S(1)}, bf16[256,256]{1,0:T(8,128)(2,1)}, u32[]{:S(2)}) copy-start(bf16[256,256]{1,0:T(8,128)(2,1)} %emb.1) | copy-start | bytes 393220
  3.8 0.9 %copy-start.2 = (bf16[256,256]{1,0:T(8,128)(2,1)S(1)}, bf16[256,256]{1,0:T(8,128)(2,1)}, u32[]{:S(2)}) copy-start(bf16[256,256]{1,0:T(8,128)(2,1)} %uval.1) | copy-start | bytes 393220
  4.7 0.9 %copy-start.3 = (bf16[256,256]{1,0:T(8,128)(2,1)S(1)}, bf16[256,256]{1,0:T(8,128)(2,1)}, u32[]{:S(2)}) copy-start(bf16[256,256]{1,0:T(8,128)(2,1)} %ws.1) | copy-start | bytes 393220
  5.6 0.9 %copy-start.4 = (bf16[256,256]{1,0:T(8,128)(2,1)S(1)}, bf16[256,256]{1,0:T(8,128)(2,1)}, u32[]{:S(2)}) copy-start(bf16[256,256]{1,0:T(8,128)(2,1)} %wi.1) | copy-start | bytes 393220
  6.5 0.7 copy-start.5
  7.2 0.7 copy-start.6
  7.9 0.7 copy-start.7
  8.6 0.7 copy-start.8

commit v2 on v1

--- a/solution.py
+++ b/solution.py
@@ -16,8 +16,9 @@
 D = 256
 NL = 1024
 ORDER = [8] + [s * d for d in range(7, 0, -1) for s in (1, -1)] + [0]
-UGRP, HGRP = 4, 2
-
+UGRP, HGRP = 4, 4
+RAT = 3
+HALF = D // 2
 
 def owner_of(x, z, k):
     return (x * NZ + z) * NK + k
@@ -57,8 +58,9 @@
 
 
 def kernel(
-    cnt, aff, emb, adj, uval, udst, utgt, srow, sdst, ws, wi,
+    cnt_h, aff_h, ints_h, emb_h, adj, uval_h, ws_h, wi_h,
     out,
+    cnt, aff, ints, emb, uval, ws, wi, in_sem,
     tile, us, uz, ur, ts, tz, tr, hs, hz, hr, halo, tmat, ps, pr, own,
     adj_sem, us_s, ts_s, hs_s, uz_r, tz_r, hz_r, loc,
     ur_s, tr_s, hr_s, ur_r, tr_r, hr_r, loc2, p_s, p_r,
@@ -74,6 +76,16 @@
         return lax.rem(x + i // NK, NX), lax.rem(k + i % NK, NK)
 
     adj_copy = pltpu.make_async_copy(adj, tile, adj_sem)
+    inputs = [
+        pltpu.make_async_copy(src, dst, in_sem.at[i])
+        for i, (src, dst) in enumerate(
+            (
+                (ints_h, ints), (uval_h, uval), (cnt_h, cnt), (aff_h, aff), (emb_h, emb), (ws_h, ws), (wi_h, wi),
+            )
+        )
+    ]
+    for copy in inputs:
+        copy.start()
     adj_copy.start()
 
     barrier = pltpu.get_barrier_semaphore()
@@ -85,7 +97,11 @@
     for dev in greeted:
         pl.semaphore_signal(barrier, inc=1, device_id=dev, device_id_type=MESH)
 
-    dest = udst[...]
+    for copy in inputs[:3]:
+        copy.wait()
+    udst, utgt = ints[:, 0:256], ints[:, 256:512]
+    srow, sdst = ints[:, 512:1024], ints[:, 1024:1536]
+    dest = udst
     live = iota(dest.shape, 1) < cnt[0]
     rank = ranks(dest, live)
     zz, qq = split_owner(dest)
@@ -94,7 +110,7 @@
     vals = uval[...]
     stacked = jnp.concatenate([vals[:, :128], vals[:, 128:]], axis=0)
     us[...] = dot(onehot(NZ * NQ * 8, slot2), stacked).astype(BF16).reshape(NZ, NQ, 8, 128)
-    tgt = utgt[...] + 1
+    tgt = utgt + 1
     row_z = jnp.where(jnp.logical_and(iota((NZ, dest.shape[1]), 0) == zz, live), 1.0, 0.0)
     lane_q = onehot(128, qq * CAPU + rank)
     hi = (row_z * jnp.right_shift(tgt, 6).astype(F32)).astype(BF16)
@@ -124,22 +140,28 @@
     for copy in locals_:
         copy.start()
 
-    dest = sdst[...]
+    for copy in inputs[3:]:
+        copy.wait()
+    dest = sdst
     rank = ranks(dest, None)
     zz, qq = split_owner(dest)
     place = onehot(OWNERS * CAPR, zz * (NQ * CAPR) + qq * CAPR + rank)
-    pick = dot_t(place, onehot(D, srow[...])).astype(BF16)
-    rows = dot(pick, emb[...]).reshape(OWNERS, CAPR, D)
-    hs[...] = (
-        jnp.concatenate([rows[:, :, :128], rows[:, :, 128:]], axis=1)
-        .astype(BF16)
-        .reshape(NZ, NQ, 2 * CAPR, 128)
-    )
-    hcopies = [zcopy(hs, hz, hs_s, hz_r, s) for s in range(NZ - 1)]
-    for s in range(NZ - 1):
-        hcopies[s].start()
-    locals_.append(pltpu.make_async_copy(hs.at[z], hz.at[NZ - 1], loc.at[2]))
-    locals_[2].start()
+    pick = dot_t(place, onehot(D, srow)).astype(BF16)
+    rows = dot(pick, emb[...]).astype(BF16)
+    for h in (0, 1):
+        hs[h] = rows[:, h * HALF : (h + 1) * HALF].reshape(NZ, NQ, CAPR, HALF)
+    hcopies = [
+        [zcopy(hs.at[h], hz.at[h], hs_s.at[h], hz_r.at[h], s) for s in range(NZ - 1)] for h in (0, 1)
+    ]
+    for h in (0, 1):
+        locals_.append(pltpu.make_async_copy(hs.at[h, z], hz.at[h, NZ - 1], loc.at[2 + h]))
+        locals_[2 + h].start()
+
+    def send_half(h):
+        for s in range(NZ - 1):
+            hcopies[h][s].start()
+
+    send_half(0)
 
     def forward(src, dst, send, recv, grp, g, copies, local):
         steps = pl.ds(g, grp)
@@ -167,6 +189,8 @@
     own_t.start()
     for g in range(0, NZ, UGRP):
         forward(uz, ur, ur_s, ur_r, UGRP, g, ucopies, locals_[0])
+        if g == RAT * UGRP:
+            send_half(1)
     own_u = pltpu.make_async_copy(uz.at[:, q], ur.at[q], loc2.at[1])
     own_u.start()
 
@@ -210,52 +234,62 @@
             delta = dot(onehot(256, row_of - b * 256), values)
             tile[at] = (tile[at].astype(F32) + delta).astype(BF16)
 
-    for g in range(0, NZ, HGRP):
-        forward(hz, hr, hr_s, hr_r, HGRP, g, hcopies, locals_[2])
-    own_h = pltpu.make_async_copy(hz.at[:, q], hr.at[q], loc2.at[2])
-    own_h.start()
-    own_h.wait()
-    for g in range(NZ // HGRP):
-        some = hr.at[pl.ds(0, NQ - 1), pl.ds(g * HGRP, HGRP)]
-        pltpu.make_async_copy(some, some, hr_r.at[g]).wait()
-        for s in range(g * HGRP, (g + 1) * HGRP):
-            zs = lax.rem(z - ORDER[s] + NZ, NZ)
-            for xs in range(NX):
-                a = hr[xs * NK, s].astype(F32)
-                b = hr[xs * NK + 1, s].astype(F32)
-                at = pl.ds(pl.multiple_of((xs * NZ + zs) * 16, 16), 16)
-                halo[at, 0:128] = jnp.concatenate([a[:8], b[:8]], axis=0).astype(BF16)
-                halo[at, 128:256] = jnp.concatenate([a[8:], b[8:]], axis=0).astype(BF16)
-
-    for i in (2, 1, 3, 0):
-        cc = lax.rem(c + i, NC)
-        block = tile[pl.ds(pl.multiple_of(cc * 256, 256), 256), :]
-        share = dot(block, halo[...]).astype(BF16)
-        if i == 0:
-            own[...] = share
-        else:
-            ps[i - 1] = share
-            pltpu.make_async_remote_copy(
-                ps.at[i - 1], pr.at[i - 1], p_s, p_r, device_id=(me, cc), device_id_type=MESH
-            ).start()
-
-    some = hr.at[pl.ds(0, NQ - 1)]
-    pltpu.make_async_copy(some, some, hr_s).wait()
-    for src, sem in ((us, us_s), (ts, ts_s), (hs, hs_s)):
+    def half_product(h):
+        for g in range(0, NZ, HGRP):
+            forward(
+                hz.at[h], hr.at[h], hr_s.at[h], hr_r.at[h], HGRP, g, hcopies[h], locals_[2 + h]
+            )
+        own_h = pltpu.make_async_copy(hz.at[h, :, q], hr.at[h, q], loc2.at[2 + h])
+        own_h.start()
+        own_h.wait()
+        for g in range(NZ // HGRP):
+            some = hr.at[h, pl.ds(0, NQ - 1), pl.ds(g * HGRP, HGRP)]
+            pltpu.make_async_copy(some, some, hr_r.at[h, g]).wait()
+            for s in range(g * HGRP, (g + 1) * HGRP):
+                zs = lax.rem(z - ORDER[s] + NZ, NZ)
+                for xs in range(NX):
+                    pair = [hr[h, xs * NK + kk, s].astype(F32) for kk in range(NK)]
+                    at = pl.ds(pl.multiple_of((xs * NZ + zs) * 16, 16), 16)
+                    halo[h, at, :] = jnp.concatenate(pair, axis=0).astype(BF16)
+        for i in (2, 1, 3, 0):
+            cc = lax.rem(c + i, NC)
+            block = tile[pl.ds(pl.multiple_of(cc * 256, 256), 256), :]
+            share = dot(block, halo[h]).astype(BF16)
+            if i == 0:
+                own[h] = share
+            else:
+                ps[h, i - 1] = share
+                pltpu.make_async_remote_copy(
+                    ps.at[h, i - 1], pr.at[h, i - 1], p_s.at[h], p_r.at[h],
+                    device_id=(me, cc), device_id_type=MESH,
+                ).start()
+
+    half_product(0)
+    half_product(1)
+
+    preact = jnp.zeros((256, D), F32)
+    for h in (0, 1):
+        pltpu.make_async_copy(pr.at[h], pr.at[h], p_r.at[h]).wait()
+        neighbours = own[h].astype(F32)
+        for i in range(NC - 1):
+            neighbours = neighbours + pr[h, i].astype(F32)
+        at = pl.ds(h * HALF, HALF)
+        wide = emb[:, at].astype(F32)
+        self_sum = (neighbours + wide).astype(BF16)
+        inter = (neighbours * wide).astype(BF16)
+        preact = preact + dot(self_sum, ws[at, :]) + dot(inter, wi[at, :])
+    layer = jnp.where(preact >= 0, preact, 0.2 * preact)
+    out[...] = jnp.where(aff[0] > 0, layer, emb[...].astype(F32)).astype(BF16)
+
+    for h in (0, 1):
+        some = hr.at[h, pl.ds(0, NQ - 1)]
+        pltpu.make_async_copy(some, some, hr_s.at[h]).wait()
+        some = hs.at[h, pl.ds(0, NZ - 1)]
+        pltpu.make_async_copy(some, some, hs_s.at[h]).wait()
+        pltpu.make_async_copy(ps.at[h], ps.at[h], p_s.at[h]).wait()
+    for src, sem in ((us, us_s), (ts, ts_s)):
         some = src.at[pl.ds(0, NZ - 1)]
         pltpu.make_async_copy(some, some, sem).wait()
-    pltpu.make_async_copy(pr, pr, p_r).wait()
-
-    neighbours = own[...].astype(F32)
-    for i in range(NC - 1):
-        neighbours = neighbours + pr[i].astype(F32)
-    wide = emb[...].astype(F32)
-    self_sum = (neighbours + wide).astype(BF16)
-    inter = (neighbours * wide).astype(BF16)
-    preact = dot(self_sum, ws[...]) + dot(inter, wi[...])
-    layer = jnp.where(preact >= 0, preact, 0.2 * preact)
-    out[...] = jnp.where(aff[0] > 0, layer, wide).astype(BF16)
-    pltpu.make_async_copy(ps, ps, p_s).wait()
 
 
 def per_device(
@@ -263,17 +297,25 @@
     send_row, send_dest, affected, w_self, w_inter,
 ):
     v = pl.BlockSpec(memory_space=pltpu.VMEM)
-    s = pl.BlockSpec(memory_space=pltpu.SMEM)
-    a = pl.BlockSpec(memory_space=pl.ANY)
+    a = pl.BlockSpec(memory_space=pltpu.HBM)
     vm = pltpu.VMEM
     dma = pltpu.SemaphoreType.DMA
     u, r = upd_dest.shape[0], send_dest.shape[0]
+    ints = jnp.concatenate(
+        [
+            upd_dest.reshape(1, u), upd_target.reshape(1, u), send_row.reshape(1, r),
+            send_dest.reshape(1, r),
+        ],
+        axis=1,
+    )
     return pl.pallas_call(
         kernel,
         out_shape=jax.ShapeDtypeStruct((D, D), BF16),
-        in_specs=[s, s, v, a, v, v, v, v, v, v, v],
+        in_specs=[a] * 8,
         out_specs=v,
         scratch_shapes=[
+            pltpu.SMEM((1,), I32), pltpu.SMEM((1,), I32), vm((1, 1536), I32), vm((D, D), BF16), vm((u, D), BF16), vm((D, D), BF16), vm((D, D), BF16),
+            dma((7,)),
             vm((NL, NL), BF16),
             vm((NZ, NQ, 8, 128), BF16),
             vm((NZ, NQ, 8, 128), BF16),
@@ -281,25 +323,22 @@
             vm((NZ, 1, 128), I32),
             vm((NZ, 1, 128), I32),
             vm((NQ, NZ, 1, 128), I32),
-            vm((NZ, NQ, 16, 128), BF16),
-            vm((NZ, NQ, 16, 128), BF16),
-            vm((NQ, NZ, 16, 128), BF16),
-            vm((OWNERS * CAPR, D), BF16),
+            vm((2, NZ, NQ, CAPR, HALF), BF16),
+            vm((2, NZ, NQ, CAPR, HALF), BF16),
+            vm((2, NQ, NZ, CAPR, HALF), BF16),
+            vm((2, OWNERS * CAPR, HALF), BF16),
             vm((128, 128), I32),
-            vm((NC - 1, 256, 256), BF16),
-            vm((NC - 1, 256, 256), BF16),
-            vm((256, 256), BF16),
-            dma, dma, dma, dma, dma((NZ,)), dma((NZ,)), dma((NZ,)), dma((3,)),
-            dma, dma, dma, dma((NZ // UGRP,)), dma, dma((NZ // HGRP,)), dma((3,)), dma, dma,
+            vm((2, NC - 1, 256, HALF), BF16),
+            vm((2, NC - 1, 256, HALF), BF16),
+            vm((2, 256, HALF), BF16),
+            dma, dma, dma, dma((2,)), dma((NZ,)), dma((NZ,)), dma((2, NZ)), dma((4,)),
+            dma, dma, dma((2,)), dma((NZ // UGRP,)), dma, dma((2, NZ // HGRP)), dma((4,)),
+            dma((2,)), dma((2,)),
         ],
         compiler_params=pltpu.CompilerParams(
-            collective_id=0, has_side_effects=True, vmem_limit_bytes=48 * 2**20
+            collective_id=0, has_side_effects=True, vmem_limit_bytes=3440 * 2**14
         ),
-    )(
-        upd_count, affected, embeddings, adjacency, upd_vals,
-        upd_dest.reshape(1, u), upd_target.reshape(1, u),
-        send_row.reshape(1, r), send_dest.reshape(1, r), w_self, w_inter,
-    )
+    )(upd_count, affected, ints, embeddings, adjacency, upd_vals, w_self, w_inter)
 
 
 def solution(mesh):

time: 77.5 us -> 67.4 us (0.87)
  local copies, waits for them, and re-layouts: 8.58 us -> 0.66 us
  Pallas kernels: 67.3 us -> 64.5 us
    unnamed x19 -> x1, local copies, waits for them, and re-layouts: 8.58 us -> 0.66 us
    pallas_call x1, Pallas kernels: 67.3 us -> 64.5 us  [per_device(): pl.pallas_call(kernel, out_shape=jax.ShapeDtypeStruct((D, D), BF16), in_s...]
where the time goes in v2:
time: 67.4 us; the launch traced here: 67.2 us
  Pallas kernels  64.5 us (96%)
  between operations  1.31 us (2%)
  other arithmetic  0.73 us (1%)
    pallas_call x1, Pallas kernels, per_device(): pl.pallas_call(kernel, out_shape=jax.ShapeDtypeStruct((D, D), BF16), in_s...  64.5 us

profile of v2, /device:TPU:1, one launch (start us, length us, event | category | flops | bytes accessed | tf_op | source)
XLA Modules:
  0.0 67.2 jit_solution(8259906905843571536)
XLA Ops:
  1.3 0.7 %pad_add_fusion.ints_h = s32[1,1536]{1,0:T(1,128)S(1)} fusion(s32[1,512]{1,0:T(1,128)} %bitcast.4, s32[1,512]{1,0:T(1,128)} %bitcast.5, s32[1,256]{1,0:T(1,128)} %bitcast.6, s32[1,256]{1,0:T(1,128)} %bitcast.7), kind=kLoop, calls=%fused_computation | loop fusion | flops 4608 | bytes 12288 | tf_op jit(solution)/shard_map/concatenate | solution.py:304
  2.0 64.5 %shard_map.109 = bf16[256,256]{1,0:T(8,128)(2,1)S(1)} custom-call(s32[1]{0:T(128)S(6)} %copy.13.cnt_h, s32[1]{0:T(128)S(6)} %copy.14.aff_h, s32[1,1536]{1,0:T(1,128)S(1)} %pad_add_fusion.ints_h, bf16[256,256]{1,0:T(8,128)(2,1)} %emb_h.1, bf16[1024,1024]{1,0:T(8,128)(2,1)} %adj.1, bf16[256,256]{1,0:T(8,128)(2,1)} %uval_h.1, bf16[256,256]{1,0:T(8,128)(2,1)} %ws_h.1, ...), custom_call_target="tpu_custom_call" | custom-call | tf_op jit(solution)/shard_map/pallas_call | solution.py:311
  66.6 0.7 copy.15

commit v3 on v2

--- a/solution.py
+++ b/solution.py
@@ -16,8 +16,7 @@
 D = 256
 NL = 1024
 ORDER = [8] + [s * d for d in range(7, 0, -1) for s in (1, -1)] + [0]
-UGRP, HGRP = 4, 4
-RAT = 3
+GROUPS = [range(0, 4), range(4, 8), range(8, 12), range(12, 15), range(15, 16)]
 HALF = D // 2
 
 def owner_of(x, z, k):
@@ -61,9 +60,9 @@
     cnt_h, aff_h, ints_h, emb_h, adj, uval_h, ws_h, wi_h,
     out,
     cnt, aff, ints, emb, uval, ws, wi, in_sem,
-    tile, us, uz, ur, ts, tz, tr, hs, hz, hr, halo, tmat, ps, pr, own,
-    adj_sem, us_s, ts_s, hs_s, uz_r, tz_r, hz_r, loc,
-    ur_s, tr_s, hr_s, ur_r, tr_r, hr_r, loc2, p_s, p_r,
+    tile, us, ur, ts, tz, tr, hs, hr, halo, tmat, ps, pr, own,
+    adj_sem, us_s, ts_s, hs_s, tz_r, loc,
+    tr_s, ur_r, tr_r, hr_r, own_t_s, p_s, p_r,
 ):
     me, c = lax.axis_index("owner"), lax.axis_index("col")
     x, z, k = me // (NZ * NK), lax.rem(me // NK, NZ), lax.rem(me, NK)
@@ -89,10 +88,12 @@
     adj_copy.start()
 
     barrier = pltpu.get_barrier_semaphore()
-    greeted = [zdev(s, 1) for s in range(NZ - 1)]
-    for i in range(1, NQ):
-        xx, kk = qdev(i)
-        greeted.append((owner_of(xx, z, kk), c))
+    greeted = []
+    for s in range(NZ):
+        for i in range(NQ):
+            if s < NZ - 1 or i:
+                xx, kk = qdev(i)
+                greeted.append((owner_of(xx, lax.rem(z + ORDER[s] + NZ, NZ), kk), c))
     greeted += [(me, lax.rem(c + i, NC)) for i in range(1, NC)]
     for dev in greeted:
         pl.semaphore_signal(barrier, inc=1, device_id=dev, device_id_type=MESH)
@@ -128,13 +129,30 @@
             device_id=dev, device_id_type=MESH,
         )
 
-    ucopies = [zcopy(us, uz, us_s, uz_r, s) for s in range(NZ - 1)]
+    def direct(src, dst, send, recv):
+        for i in (3, 5, 2, 4, 6, 7, 1, 0):
+            for s in range(NZ):
+                zz = lax.rem(z + ORDER[s] + NZ, NZ)
+                g = [g for g, steps in enumerate(GROUPS) if s in steps][0]
+                if s < NZ - 1 or i:
+                    xx, kk = qdev(i)
+                    pltpu.make_async_remote_copy(
+                        src.at[zz, xx * NK + kk], dst.at[q, s], send.at[g], recv.at[g],
+                        device_id=(owner_of(xx, zz, kk), c), device_id_type=MESH,
+                    ).start()
+
+    def wait_group(src, sem, g):
+        some = src.at[pl.ds(0, len(GROUPS[g]))]
+        if g == len(GROUPS) - 1:
+            some = src.at[0, pl.ds(0, NQ - 1)]
+        pltpu.make_async_copy(some, some, sem.at[g]).wait()
+
     tcopies = [zcopy(ts, tz, ts_s, tz_r, s) for s in range(NZ - 1)]
     for s in range(NZ - 1):
         tcopies[s].start()
-        ucopies[s].start()
+    direct(us, ur, us_s, ur_r)
     locals_ = [
-        pltpu.make_async_copy(us.at[z], uz.at[NZ - 1], loc.at[0]),
+        pltpu.make_async_copy(us.at[z, q], ur.at[q, NZ - 1], loc.at[0]),
         pltpu.make_async_copy(ts.at[z], tz.at[NZ - 1], loc.at[1]),
     ]
     for copy in locals_:
@@ -150,32 +168,10 @@
     rows = dot(pick, emb[...]).astype(BF16)
     for h in (0, 1):
         hs[h] = rows[:, h * HALF : (h + 1) * HALF].reshape(NZ, NQ, CAPR, HALF)
-    hcopies = [
-        [zcopy(hs.at[h], hz.at[h], hs_s.at[h], hz_r.at[h], s) for s in range(NZ - 1)] for h in (0, 1)
-    ]
+    direct(hs.at[0], hr.at[0], hs_s.at[0], hr_r.at[0])
     for h in (0, 1):
-        locals_.append(pltpu.make_async_copy(hs.at[h, z], hz.at[h, NZ - 1], loc.at[2 + h]))
+        locals_.append(pltpu.make_async_copy(hs.at[h, z, q], hr.at[h, q, NZ - 1], loc.at[2 + h]))
         locals_[2 + h].start()
-
-    def send_half(h):
-        for s in range(NZ - 1):
-            hcopies[h][s].start()
-
-    send_half(0)
-
-    def forward(src, dst, send, recv, grp, g, copies, local):
-        steps = pl.ds(g, grp)
-        for s in range(g, g + grp):
-            if s < NZ - 1:
-                copies[s].wait_recv()
-            else:
-                local.wait()
-        for i in (3, 5, 2, 4, 6, 7, 1):
-            xx, kk = qdev(i)
-            pltpu.make_async_remote_copy(
-                src.at[steps, xx * NK + kk], dst.at[q, steps], send, recv.at[g // grp],
-                device_id=(owner_of(xx, z, kk), c), device_id_type=MESH,
-            ).start()
 
     for s in range(NZ - 1):
         tcopies[s].wait_recv()
@@ -185,25 +181,16 @@
         pltpu.make_async_remote_copy(
             tz, tr.at[q], tr_s, tr_r, device_id=(owner_of(xx, z, kk), c), device_id_type=MESH
         ).start()
-    own_t = pltpu.make_async_copy(tz, tr.at[q], loc2.at[0])
+    own_t = pltpu.make_async_copy(tz, tr.at[q], own_t_s)
     own_t.start()
-    for g in range(0, NZ, UGRP):
-        forward(uz, ur, ur_s, ur_r, UGRP, g, ucopies, locals_[0])
-        if g == RAT * UGRP:
-            send_half(1)
-    own_u = pltpu.make_async_copy(uz.at[:, q], ur.at[q], loc2.at[1])
-    own_u.start()
-
+    direct(hs.at[1], hr.at[1], hs_s.at[1], hr_r.at[1])
     own_t.wait()
     some = tr.at[pl.ds(0, NQ - 1)]
     pltpu.make_async_copy(some, some, tr_r).wait()
     pltpu.make_async_copy(some, some, tr_s).wait()
-    own_u.wait()
-    for g in range(NZ // UGRP):
-        some = ur.at[pl.ds(0, NQ - 1), pl.ds(g * UGRP, UGRP)]
-        pltpu.make_async_copy(some, some, ur_r.at[g]).wait()
-    some = ur.at[pl.ds(0, NQ - 1)]
-    pltpu.make_async_copy(some, some, ur_s).wait()
+    locals_[0].wait()
+    for g in range(len(GROUPS)):
+        wait_group(us, ur_r, g)
 
     for i in range(OWNERS):
         tmat[i : i + 1] = tr[i // NZ, i % NZ]
@@ -235,17 +222,10 @@
             tile[at] = (tile[at].astype(F32) + delta).astype(BF16)
 
     def half_product(h):
-        for g in range(0, NZ, HGRP):
-            forward(
-                hz.at[h], hr.at[h], hr_s.at[h], hr_r.at[h], HGRP, g, hcopies[h], locals_[2 + h]
-            )
-        own_h = pltpu.make_async_copy(hz.at[h, :, q], hr.at[h, q], loc2.at[2 + h])
-        own_h.start()
-        own_h.wait()
-        for g in range(NZ // HGRP):
-            some = hr.at[h, pl.ds(0, NQ - 1), pl.ds(g * HGRP, HGRP)]
-            pltpu.make_async_copy(some, some, hr_r.at[h, g]).wait()
-            for s in range(g * HGRP, (g + 1) * HGRP):
+        locals_[2 + h].wait()
+        for g, steps in enumerate(GROUPS):
+            wait_group(hs.at[h], hr_r.at[h], g)
+            for s in steps:
                 zs = lax.rem(z - ORDER[s] + NZ, NZ)
                 for xs in range(NX):
                     pair = [hr[h, xs * NK + kk, s].astype(F32) for kk in range(NK)]
@@ -282,14 +262,13 @@
     out[...] = jnp.where(aff[0] > 0, layer, emb[...].astype(F32)).astype(BF16)
 
     for h in (0, 1):
-        some = hr.at[h, pl.ds(0, NQ - 1)]
-        pltpu.make_async_copy(some, some, hr_s.at[h]).wait()
-        some = hs.at[h, pl.ds(0, NZ - 1)]
-        pltpu.make_async_copy(some, some, hs_s.at[h]).wait()
+        for g in range(len(GROUPS)):
+            wait_group(hs.at[h], hs_s.at[h], g)
         pltpu.make_async_copy(ps.at[h], ps.at[h], p_s.at[h]).wait()
-    for src, sem in ((us, us_s), (ts, ts_s)):
-        some = src.at[pl.ds(0, NZ - 1)]
-        pltpu.make_async_copy(some, some, sem).wait()
+    for g in range(len(GROUPS)):
+        wait_group(us, us_s, g)
+    some = ts.at[pl.ds(0, NZ - 1)]
+    pltpu.make_async_copy(some, some, ts_s).wait()
 
 
 def per_device(
@@ -300,6 +279,7 @@
     a = pl.BlockSpec(memory_space=pltpu.HBM)
     vm = pltpu.VMEM
     dma = pltpu.SemaphoreType.DMA
+    n = len(GROUPS)
     u, r = upd_dest.shape[0], send_dest.shape[0]
     ints = jnp.concatenate(
         [
@@ -318,12 +298,10 @@
             dma((7,)),
             vm((NL, NL), BF16),
             vm((NZ, NQ, 8, 128), BF16),
-            vm((NZ, NQ, 8, 128), BF16),
             vm((NQ, NZ, 8, 128), BF16),
             vm((NZ, 1, 128), I32),
             vm((NZ, 1, 128), I32),
             vm((NQ, NZ, 1, 128), I32),
-            vm((2, NZ, NQ, CAPR, HALF), BF16),
             vm((2, NZ, NQ, CAPR, HALF), BF16),
             vm((2, NQ, NZ, CAPR, HALF), BF16),
             vm((2, OWNERS * CAPR, HALF), BF16),
@@ -331,9 +309,8 @@
             vm((2, NC - 1, 256, HALF), BF16),
             vm((2, NC - 1, 256, HALF), BF16),
             vm((2, 256, HALF), BF16),
-            dma, dma, dma, dma((2,)), dma((NZ,)), dma((NZ,)), dma((2, NZ)), dma((4,)),
-            dma, dma, dma((2,)), dma((NZ // UGRP,)), dma, dma((2, NZ // HGRP)), dma((4,)),
-            dma((2,)), dma((2,)),
+            dma, dma((n,)), dma, dma((2, n)), dma((NZ,)), dma((4,)),
+            dma, dma((n,)), dma, dma((2, n)), dma, dma((2,)), dma((2,)),
         ],
         compiler_params=pltpu.CompilerParams(
             collective_id=0, has_side_effects=True, vmem_limit_bytes=3440 * 2**14

time: 67.4 us -> 64.6 us (0.958)
  Pallas kernels: 64.5 us -> 61.6 us
    pallas_call x1, Pallas kernels: 64.5 us -> 61.6 us  [per_device(): pl.pallas_call(kernel, out_shape=jax.ShapeDtypeStruct((D, D), BF16), in_s...]
where the time goes in v3:
time: 64.6 us; the launch traced here: 64.3 us
  Pallas kernels  61.6 us (95%)
  between operations  1.31 us (2%)
  other arithmetic  0.73 us (1%)
  local copies, waits for them, and re-layouts  0.66 us (1%)
    pallas_call x1, Pallas kernels, per_device(): pl.pallas_call(kernel, out_shape=jax.ShapeDtypeStruct((D, D), BF16), in_s...  61.6 us

profile of v3, /device:TPU:1, one launch (start us, length us, event | category | flops | bytes accessed | tf_op | source)
XLA Modules:
  0.0 64.3 jit_solution(10759440667269951787)
XLA Ops:
  1.3 0.7 %pad_add_fusion.ints_h = s32[1,1536]{1,0:T(1,128)S(1)} fusion(s32[1,512]{1,0:T(1,128)} %bitcast.4, s32[1,512]{1,0:T(1,128)} %bitcast.5, s32[1,256]{1,0:T(1,128)} %bitcast.6, s32[1,256]{1,0:T(1,128)} %bitcast.7), kind=kLoop, calls=%fused_computation | loop fusion | flops 4608 | bytes 12288 | tf_op jit(solution)/shard_map/concatenate | solution.py:284
  2.0 61.6 %shard_map.109 = bf16[256,256]{1,0:T(8,128)(2,1)S(1)} custom-call(s32[1]{0:T(128)S(6)} %copy.13.cnt_h, s32[1]{0:T(128)S(6)} %copy.14.aff_h, s32[1,1536]{1,0:T(1,128)S(1)} %pad_add_fusion.ints_h, bf16[256,256]{1,0:T(8,128)(2,1)} %emb_h.1, bf16[1024,1024]{1,0:T(8,128)(2,1)} %adj.1, bf16[256,256]{1,0:T(8,128)(2,1)} %uval_h.1, bf16[256,256]{1,0:T(8,128)(2,1)} %ws_h.1, ...), custom_call_target="tpu_custom_call" | custom-call | tf_op jit(solution)/shard_map/pallas_call | solution.py:291
  63.6 0.7 %copy.15 = bf16[256,256]{1,0:T(8,128)(2,1)} copy(bf16[256,256]{1,0:T(8,128)(2,1)S(1)} %shard_map.109) | data formatting | bytes 262144

commit v4 on v3

--- a/solution.py
+++ b/solution.py
@@ -17,6 +17,8 @@
 NL = 1024
 ORDER = [8] + [s * d for d in range(7, 0, -1) for s in (1, -1)] + [0]
 GROUPS = [range(0, 4), range(4, 8), range(8, 12), range(12, 15), range(15, 16)]
+PIECES = 2
+PIECE = 256 // PIECES
 HALF = D // 2
 
 def owner_of(x, z, k):
@@ -130,7 +132,7 @@
         )
 
     def direct(src, dst, send, recv):
-        for i in (3, 5, 2, 4, 6, 7, 1, 0):
+        for i in (5, 3, 7, 1, 4, 2, 6, 0):
             for s in range(NZ):
                 zz = lax.rem(z + ORDER[s] + NZ, NZ)
                 g = [g for g, steps in enumerate(GROUPS) if s in steps][0]
@@ -231,40 +233,44 @@
                     pair = [hr[h, xs * NK + kk, s].astype(F32) for kk in range(NK)]
                     at = pl.ds(pl.multiple_of((xs * NZ + zs) * 16, 16), 16)
                     halo[h, at, :] = jnp.concatenate(pair, axis=0).astype(BF16)
-        for i in (2, 1, 3, 0):
-            cc = lax.rem(c + i, NC)
-            block = tile[pl.ds(pl.multiple_of(cc * 256, 256), 256), :]
-            share = dot(block, halo[h]).astype(BF16)
-            if i == 0:
-                own[h] = share
-            else:
-                ps[h, i - 1] = share
-                pltpu.make_async_remote_copy(
-                    ps.at[h, i - 1], pr.at[h, i - 1], p_s.at[h], p_r.at[h],
-                    device_id=(me, cc), device_id_type=MESH,
-                ).start()
+        for b in range(PIECES):
+            for i in (2, 1, 3, 0):
+                cc = lax.rem(c + i, NC)
+                at = pl.ds(pl.multiple_of(cc * 256 + b * PIECE, PIECE), PIECE)
+                share = dot(tile[at, :], halo[h]).astype(BF16)
+                if i == 0:
+                    own[h, b] = share
+                else:
+                    ps[h, b, i - 1] = share
+                    pltpu.make_async_remote_copy(
+                        ps.at[h, b, i - 1], pr.at[h, b, i - 1], p_s.at[h, b], p_r.at[h, b],
+                        device_id=(me, cc), device_id_type=MESH,
+                    ).start()
 
     half_product(0)
     half_product(1)
 
-    preact = jnp.zeros((256, D), F32)
-    for h in (0, 1):
-        pltpu.make_async_copy(pr.at[h], pr.at[h], p_r.at[h]).wait()
-        neighbours = own[h].astype(F32)
-        for i in range(NC - 1):
-            neighbours = neighbours + pr[h, i].astype(F32)
-        at = pl.ds(h * HALF, HALF)
-        wide = emb[:, at].astype(F32)
-        self_sum = (neighbours + wide).astype(BF16)
-        inter = (neighbours * wide).astype(BF16)
-        preact = preact + dot(self_sum, ws[at, :]) + dot(inter, wi[at, :])
-    layer = jnp.where(preact >= 0, preact, 0.2 * preact)
-    out[...] = jnp.where(aff[0] > 0, layer, emb[...].astype(F32)).astype(BF16)
+    for b in range(PIECES):
+        rows = pl.ds(b * PIECE, PIECE)
+        preact = jnp.zeros((PIECE, D), F32)
+        for h in (0, 1):
+            pltpu.make_async_copy(pr.at[h, b], pr.at[h, b], p_r.at[h, b]).wait()
+            neighbours = own[h, b].astype(F32)
+            for i in range(NC - 1):
+                neighbours = neighbours + pr[h, b, i].astype(F32)
+            at = pl.ds(h * HALF, HALF)
+            wide = emb[rows, at].astype(F32)
+            self_sum = (neighbours + wide).astype(BF16)
+            inter = (neighbours * wide).astype(BF16)
+            preact = preact + dot(self_sum, ws[at, :]) + dot(inter, wi[at, :])
+        layer = jnp.where(preact >= 0, preact, 0.2 * preact)
+        out[rows, :] = jnp.where(aff[0] > 0, layer, emb[rows, :].astype(F32)).astype(BF16)
 
     for h in (0, 1):
         for g in range(len(GROUPS)):
             wait_group(hs.at[h], hs_s.at[h], g)
-        pltpu.make_async_copy(ps.at[h], ps.at[h], p_s.at[h]).wait()
+        for b in range(PIECES):
+            pltpu.make_async_copy(ps.at[h, b], ps.at[h, b], p_s.at[h, b]).wait()
     for g in range(len(GROUPS)):
         wait_group(us, us_s, g)
     some = ts.at[pl.ds(0, NZ - 1)]
@@ -306,11 +312,11 @@
             vm((2, NQ, NZ, CAPR, HALF), BF16),
             vm((2, OWNERS * CAPR, HALF), BF16),
             vm((128, 128), I32),
-            vm((2, NC - 1, 256, HALF), BF16),
-            vm((2, NC - 1, 256, HALF), BF16),
-            vm((2, 256, HALF), BF16),
+            vm((2, PIECES, NC - 1, PIECE, HALF), BF16),
+            vm((2, PIECES, NC - 1, PIECE, HALF), BF16),
+            vm((2, PIECES, PIECE, HALF), BF16),
             dma, dma((n,)), dma, dma((2, n)), dma((NZ,)), dma((4,)),
-            dma, dma((n,)), dma, dma((2, n)), dma, dma((2,)), dma((2,)),
+            dma, dma((n,)), dma, dma((2, n)), dma, dma((2, PIECES)), dma((2, PIECES)),
         ],
         compiler_params=pltpu.CompilerParams(
             collective_id=0, has_side_effects=True, vmem_limit_bytes=3440 * 2**14

time: 64.6 us -> 64.5 us (level)
    pallas_call x1, Pallas kernels: 61.6 us -> 61 us  [per_device(): pl.pallas_call(kernel, out_shape=jax.ShapeDtypeStruct((D, D), BF16), in_s...]
where the time goes in v4:
time: 64.5 us; the launch traced here: 63.6 us
  Pallas kernels  61 us (95%)
  between operations  1.31 us (2%)
  other arithmetic  0.73 us (1%)
  local copies, waits for them, and re-layouts  0.66 us (1%)
    pallas_call x1, Pallas kernels, per_device(): pl.pallas_call(kernel, out_shape=jax.ShapeDtypeStruct((D, D), BF16), in_s...  61 us

profile of v4, /device:TPU:1, one launch (start us, length us, event | category | flops | bytes accessed | tf_op | source)
XLA Modules:
  0.0 63.6 jit_solution(3721877907955753845)
XLA Ops:
  1.3 0.7 %pad_add_fusion.ints_h = s32[1,1536]{1,0:T(1,128)S(1)} fusion(s32[1,512]{1,0:T(1,128)} %bitcast.4, s32[1,512]{1,0:T(1,128)} %bitcast.5, s32[1,256]{1,0:T(1,128)} %bitcast.6, s32[1,256]{1,0:T(1,128)} %bitcast.7), kind=kLoop, calls=%fused_computation | loop fusion | flops 4608 | bytes 12288 | tf_op jit(solution)/shard_map/concatenate | solution.py:290
  2.0 61.0 %shard_map.109 = bf16[256,256]{1,0:T(8,128)(2,1)S(1)} custom-call(s32[1]{0:T(128)S(6)} %copy.13.cnt_h, s32[1]{0:T(128)S(6)} %copy.14.aff_h, s32[1,1536]{1,0:T(1,128)S(1)} %pad_add_fusion.ints_h, bf16[256,256]{1,0:T(8,128)(2,1)} %emb_h.1, bf16[1024,1024]{1,0:T(8,128)(2,1)} %adj.1, bf16[256,256]{1,0:T(8,128)(2,1)} %uval_h.1, bf16[256,256]{1,0:T(8,128)(2,1)} %ws_h.1, ...), custom_call_target="tpu_custom_call" | custom-call | tf_op jit(solution)/shard_map/pallas_call | solution.py:297
  63.0 0.7 %copy.15 = bf16[256,256]{1,0:T(8,128)(2,1)} copy(bf16[256,256]{1,0:T(8,128)(2,1)S(1)} %shard_map.109) | data formatting | bytes 262144
